TPU v7x, 512 devices: a whole 4x4x16 slice. The times are simulated.
512 devices in a mesh: row: 32 (over x, y, core), col: 16 (over z).
Axes of the slice: x: 4, y: 4, z: 16, core: 2. Of those that a mesh axis runs over, the one named last changes fastest.
Arguments:
- row_desc: bfloat16 [65536, 1024], P(('row', 'col')), may hold values from -80 to 80
- row_scale: float32 [65536], P('row'), may hold values from 0.3 to 0.9
- col_desc: bfloat16 [32768, 1024], P('col'), may hold values from -80 to 80
- col_scale: bfloat16 [32768], P('col'), may hold values from 0.29882812 to 0.8984375
- probe: bfloat16 [32768, 128], P('col'), may hold values from -5 to 5
- pair_list: int32 [64, 24], P('row'), may hold values from -1 to 31, as said below
Outputs:
- basis_out: float32 [65536, 128], P(('row', 'col'))
- r_factor: float32 [128, 128], replicated
Inputs may be any that keep to these rules, and one draw needn't show every extreme that they name: Each row of pair_list holds distinct column block numbers first and -1 in the remaining slots; each row block lists between 16 and 24 blocks, and row block 0 lists 24. Some column blocks are listed far more often than others.
All inputs are finite; a program needn't handle non-finite values.
Results may differ from a plain program's by a relative error of at most 0.0061.
Values may be sent and summed in bfloat16 or wider, within the bound.
A program may use at most 64 MiB of HBM per device.

v0:
```python
import jax
import jax.numpy as jnp
from jax import lax
from jax.sharding import PartitionSpec as P

BLK = 1024


def unit_rows(descriptors):
    widened = descriptors.astype(jnp.float32)
    total = jnp.sum(widened * widened, axis=1, keepdims=True)
    return (widened * lax.rsqrt(total + 1e-06)).astype(jnp.bfloat16)


def tile_sketch(row_tile, row_band, col_tile, col_band, probe_tile):
    cosine = jnp.dot(row_tile, col_tile.T, preferred_element_type=jnp.float32)
    affinity = jnp.exp((2.0 * cosine - 2.0) / (row_band[:, None] * col_band[None, :])).astype(
        jnp.bfloat16
    )
    return jnp.dot(affinity, probe_tile, preferred_element_type=jnp.float32)


def shards(row_desc, row_scale, col_desc, col_scale, probe, pair_list):
    row_unit = unit_rows(row_desc)
    gathered = lax.all_gather(row_unit, "col", axis=0, tiled=True)
    col_unit = unit_rows(col_desc)
    blocks = pair_list.shape[0]
    own_blocks = col_desc.shape[0] // BLK
    probe_width = probe.shape[1]
    column = lax.axis_index("col")
    col_count = lax.axis_size("col")
    block_ids = column * own_blocks + jnp.arange(own_blocks, dtype=jnp.int32)
    own_listed = jnp.any(pair_list[:, :, None] == block_ids[None, None, :], axis=1)
    sources = ((col_unit, probe, col_scale, own_listed),)

    def one_block(b, sketch):
        offset = b * BLK
        row_tile = lax.dynamic_slice_in_dim(gathered, offset, BLK, 0)
        row_band = lax.dynamic_slice_in_dim(row_scale, offset, BLK, 0)
        running = jnp.zeros((BLK, probe_width), jnp.float32)
        units, probes, scales, marked = sources[0]
        for q in range(own_blocks):
            col_tile = units[q * BLK : (q + 1) * BLK]
            col_band = scales[q * BLK : (q + 1) * BLK].astype(jnp.float32)
            probe_tile = probes[q * BLK : (q + 1) * BLK]

            def add_tile(current, col_tile=col_tile, col_band=col_band, probe_tile=probe_tile):
                return current + tile_sketch(row_tile, row_band, col_tile, col_band, probe_tile)

            def keep_tile(current):
                return current

            running = lax.cond(marked[b, q], add_tile, keep_tile, running)
        return lax.dynamic_update_slice_in_dim(sketch, running, offset, 0)

    sketch = lax.fori_loop(
        0, blocks, one_block, jnp.zeros((blocks * BLK, probe_width), jnp.float32)
    )
    rows_total = sketch.shape[0] * lax.axis_size("row")
    share_rows = sketch.shape[0] // col_count
    summed = lax.psum(sketch, "col")
    local_gram = jnp.dot(
        summed.T, summed, precision=lax.Precision.HIGHEST, preferred_element_type=jnp.float32
    )
    gram_sum = lax.psum(local_gram, "row")
    row_share = lax.dynamic_slice_in_dim(summed, column * share_rows, share_rows, 0)
    gram_sum = gram_sum / rows_total
    factor_low = jnp.linalg.cholesky(gram_sum)
    basis_out = jax.scipy.linalg.solve_triangular(factor_low, row_share.T, lower=True).T
    return (basis_out, factor_low.T)


def solution(mesh):
    return jax.shard_map(
        shards,
        mesh=mesh,
        in_specs=(
            P(("row", "col"), None),
            P("row"),
            P("col", None),
            P("col"),
            P("col", None),
            P("row", None),
        ),
        out_specs=(P(("row", "col"), None), P()),
        check_vma=False,
    )
```

profile of v0, /device:TPU:1, one launch (start us, length us, event | category | flops | bytes accessed | tf_op | source)
XLA Modules:
  0.0 420.0 jit_solution(12524565807274808939)
XLA Ops:
  7.2 1.1 fusion.19
  8.3 1.8 fusion.20
  10.2 1.0 compare_reduce_fusion
  11.2 3.3 fusion.17
  14.6 2.7 fusion.18
  17.3 68.2 %all-gather.2.cloned.1.call-done = bf16[2048,1024]{1,0:T(8,128)(2,1)} async-done(((bf16[128,1024]{1,0:T(8,128)(2,1)}), bf16[2048,1024]{1,0:T(8,128)(2,1)}) %all-gather.2.cloned.1.call-update) | async-done | bytes 4194320 | tf_op jit(solution)/shard_map/all_gather | solution.py:25
  85.5 1.1 broadcast_in_dim.3
  86.7 28.6 %while.13 = (s32[]{:T(128)}, f32[2048,128]{1,0:T(8,128)}, pred[2,2]{1,0:T(4,128)(4,1)S(1)}, bf16[2048,1024]{1,0:T(8,128)(2,1)}, bf16[2048,1024]{1,0:T(8,128)(2,1...) while((s32[]{:T(128)}, f32[2048,128]{1,0:T(8,128)}, ...), condition=%wide.region_8.0_spmd, body=%wide.region_3.0_spmd.sunk | while | flops 4842457088 | bytes 15765809 | solution.py:56
  86.7 0.7 constant_dynamic-slice_fusion.5
  88.7 1.8 constant_dynamic-slice_fusion.6
  90.5 4.8 %conditional.4 = (f32[1024,128]{1,0:T(8,128)S(1)}) conditional(s32[]{:T(128)} %bitcast.20, () %tuple.56, (bf16[1024,1024]{1,0:T(8,128)(2,1)S(1)}, bf16[2048,1024]{1,0:T(8,128)(2,1)}, f32[1024]{0:T(1024)S(1)}, f32[1024]{0:T(1024)S(1)}, bf16[2048,128]{1,0:T(8,128)(2,1)S(1)}) %tuple.57), branch_computations={%region_4.0_spmd, %region_5.0_spmd} | conditional | flops 2421161984 | bytes 4988936 | solution.py:53
  90.5 4.7 %fusion.2 = f32[1024,128]{1,0:T(8,128)S(1)} fusion(bf16[1024,1024]{1,0:T(8,128)(2,1)S(1)} %get-tuple-element.168, bf16[2048,1024]{1,0:T(8,128)(2,1)} %get-tuple-element.192, f32[1024]{0:T(1024)S(1)} %get-tuple-element.171, f32[1024]{0:T(1024)S(1)} %get-tuple-element.170, bf16[2048,128]{1,0:T(8,128)(2,1)S(1)} %get-tuple-element.193), kind=kOutput, calls=%fused_computation.2 | convolution fusion | flops 2421161984 | bytes 4988928 | tf_op jit(solution)/shard_map/while/body/eval_jaxpr/cond/branch_1_fun/dot_general | solution.py:20
  95.2 4.8 %conditional.5 = (f32[1024,128]{1,0:T(8,128)S(1)}) conditional(s32[]{:T(128)} %bitcast.19, f32[1024,128]{1,0:T(8,128)S(1)} %get-tuple-element.313, (bf16[2048,1024]{1,0:T(8,128)(2,1)}, bf16[1024,1024]{1,0:T(8,128)(2,1)S(1)}, f32[1024]{0:T(1024)S(1)}, f32[1024]{0:T(1024)S(1)}, bf16[2048,128]{1,0:T(8,128)(2,1)S(1)}, ...), branch_computations={%region_6.0_spmd, %region_7.0_spmd} | conditional | flops 2421293056 | bytes 5513224 | solution.py:53
  95.3 4.8 %fusion.11 = f32[1024,128]{1,0:T(8,128)S(1)} fusion(f32[1024,128]{1,0:T(8,128)S(1)} %get-tuple-element.173, bf16[1024,1024]{1,0:T(8,128)(2,1)S(1)} %get-tuple-element.174, f32[1024]{0:T(1024)S(1)} %get-tuple-element.177, f32[1024]{0:T(1024)S(1)} %get-tuple-element.176, bf16[2048,1024]{1,0:T(8,128)(2,1)} %get-tuple-element.175, ...), kind=kOutput, calls=%fused_computation.9 | convolution fusion | flops 2421293056 | bytes 5513216 | tf_op jit(solution)/shard_map/while/body/eval_jaxpr/cond/branch_1_fun/dot_general | solution.py:20
  100.0 0.9 constant_dynamic-update-slice_fusion.2
  100.9 0.7 constant_dynamic-slice_fusion.5
  102.9 1.8 constant_dynamic-slice_fusion.6
  104.7 4.8 %conditional.4 = (f32[1024,128]{1,0:T(8,128)S(1)}) conditional(s32[]{:T(128)} %bitcast.20, () %tuple.56, (bf16[1024,1024]{1,0:T(8,128)(2,1)S(1)}, bf16[2048,1024]{1,0:T(8,128)(2,1)}, f32[1024]{0:T(1024)S(1)}, f32[1024]{0:T(1024)S(1)}, bf16[2048,128]{1,0:T(8,128)(2,1)S(1)}) %tuple.57), branch_computations={%region_4.0_spmd, %region_5.0_spmd} | conditional | flops 2421161984 | bytes 4988936 | solution.py:53
  104.7 4.7 %fusion.2 = f32[1024,128]{1,0:T(8,128)S(1)} fusion(bf16[1024,1024]{1,0:T(8,128)(2,1)S(1)} %get-tuple-element.168, bf16[2048,1024]{1,0:T(8,128)(2,1)} %get-tuple-element.192, f32[1024]{0:T(1024)S(1)} %get-tuple-element.171, f32[1024]{0:T(1024)S(1)} %get-tuple-element.170, bf16[2048,128]{1,0:T(8,128)(2,1)S(1)} %get-tuple-element.193), kind=kOutput, calls=%fused_computation.2 | convolution fusion | flops 2421161984 | bytes 4988928 | tf_op jit(solution)/shard_map/while/body/eval_jaxpr/cond/branch_1_fun/dot_general | solution.py:20
  109.5 4.8 %conditional.5 = (f32[1024,128]{1,0:T(8,128)S(1)}) conditional(s32[]{:T(128)} %bitcast.19, f32[1024,128]{1,0:T(8,128)S(1)} %get-tuple-element.313, (bf16[2048,1024]{1,0:T(8,128)(2,1)}, bf16[1024,1024]{1,0:T(8,128)(2,1)S(1)}, f32[1024]{0:T(1024)S(1)}, f32[1024]{0:T(1024)S(1)}, bf16[2048,128]{1,0:T(8,128)(2,1)S(1)}, ...), branch_computations={%region_6.0_spmd, %region_7.0_spmd} | conditional | flops 2421293056 | bytes 5513224 | solution.py:53
  109.5 4.8 %fusion.11 = f32[1024,128]{1,0:T(8,128)S(1)} fusion(f32[1024,128]{1,0:T(8,128)S(1)} %get-tuple-element.173, bf16[1024,1024]{1,0:T(8,128)(2,1)S(1)} %get-tuple-element.174, f32[1024]{0:T(1024)S(1)} %get-tuple-element.177, f32[1024]{0:T(1024)S(1)} %get-tuple-element.176, bf16[2048,1024]{1,0:T(8,128)(2,1)} %get-tuple-element.175, ...), kind=kOutput, calls=%fused_computation.9 | convolution fusion | flops 2421293056 | bytes 5513216 | tf_op jit(solution)/shard_map/while/body/eval_jaxpr/cond/branch_1_fun/dot_general | solution.py:20
  114.3 0.9 constant_dynamic-update-slice_fusion.2
  115.5 134.0 %all-reduce.3.cloned.1.call-done = f32[2048,128]{1,0:T(8,128)} async-done(((f32[2048,128]{1,0:T(8,128)}), f32[2048,128]{1,0:T(8,128)}) %all-reduce.3.cloned.1.call-update) | async-done | bytes 1048592 | tf_op jit(solution)/shard_map/psum | solution.py:61
  249.4 4.0 fusion.27
  253.5 132.9 %all-reduce.5.cloned.1.call-done = f32[128,128]{0,1:T(8,128)} async-done(((f32[128,128]{0,1:T(8,128)}), f32[128,128]{0,1:T(8,128)}) %all-reduce.5.cloned.1.call-update) | async-done | bytes 65552 | tf_op jit(solution)/shard_map/psum | solution.py:65
  386.4 0.8 broadcast_multiply_fusion
  387.3 0.9 fusion.23
  388.2 11.7 %cholesky.16 = f32[128,128]{1,0:T(8,128)S(1)} custom-call(f32[128,128]{1,0:T(8,128)S(1)} %fusion.23), custom_call_target="Cholesky" | custom-call | tf_op jit(solution)/shard_map/jit(cholesky)/cholesky | solution.py:68
  400.6 0.7 fusion.25
  401.2 0.7 copy.13
  402.0 9.8 %custom-call.7 = f32[1,128,128]{1,2,0:T(8,128)S(1)} custom-call(f32[1,128,128]{2,1,0:T(8,128)S(1)} %get-tuple-element.219), custom_call_target="InvertDiagBlocksLowerTriangular" | custom-call | tf_op jit(solution)/shard_map/jit(_solve_triangular)/triangular_solve | solution.py:69
  411.8 1.7 fusion.21
  (24 shorter events, 1.2 us)
Async XLA Ops:
  7.2 78.3 %all-gather.2.cloned.1.call-start = ((), (), s32[]{:S(2)}) async-start(), calls=%async_computation | async-start | bytes 4456448 | tf_op jit(solution)/shard_map/all_gather | solution.py:25
  10.1 239.3 %all-reduce.3.cloned.1.call-start = ((), (), s32[]{:S(2)}) async-start(), calls=%async_computation.1 | async-start | bytes 2097152 | tf_op jit(solution)/shard_map/psum | solution.py:61
  10.2 4.4 %copy-start = (bf16[2048,1024]{1,0:T(8,128)(2,1)S(1)}, bf16[2048,1024]{1,0:T(8,128)(2,1)}, u32[]{:S(2)}) copy-start(bf16[2048,1024]{1,0:T(8,128)(2,1)} %param.14) | copy-start | bytes 12582916
  14.6 72.1 %copy-start.1 = (bf16[2048]{0:T(1024)(128)(2,1)S(1)}, bf16[2048]{0:T(1024)(128)(2,1)}, u32[]{:S(2)}) copy-start(bf16[2048]{0:T(1024)(128)(2,1)} %param.15) | copy-start | bytes 12292
  14.6 72.1 %copy-start.2 = (f32[2048]{0:T(1024)S(1)}, f32[2048]{0:T(1024)}, u32[]{:S(2)}) copy-start(f32[2048]{0:T(1024)} %param.13) | copy-start | bytes 24580
  14.6 72.1 %copy-start.3 = (bf16[2048,128]{1,0:T(8,128)(2,1)S(1)}, bf16[2048,128]{1,0:T(8,128)(2,1)}, u32[]{:S(2)}) copy-start(bf16[2048,128]{1,0:T(8,128)(2,1)} %param.16) | copy-start | bytes 1572868
  115.2 271.1 %all-reduce.5.cloned.1.call-start = ((), (), s32[]{:S(2)}) async-start(), calls=%async_computation.2 | async-start | bytes 131072 | tf_op jit(solution)/shard_map/psum | solution.py:65
Sparse Core Ops, SparseCore 0:
  10.3 75.2 all-gather.1
  115.4 134.0 all-reduce.2
  253.6 132.7 all-reduce.4
where the time goes:
time: 420 us
  waiting for transfers between devices  335 us (80%)
  other arithmetic  34.5 us (8%)
  matrix products  24.7 us (6%)
  between operations  13.8 us (3%)
  local copies, waits for them, and re-layouts  8.65 us (2%)
    psum x1, waiting for transfers between devices, shards(): summed = lax.psum(sketch, 'col')  134 us
    psum x1, waiting for transfers between devices, shards(): gram_sum = lax.psum(local_gram, 'row')  133 us
    all_gather x1, waiting for transfers between devices, shards(): gathered = lax.all_gather(row_unit, 'col', axis=0, tiled=True)  68.2 us
    dot_general x4, matrix products, tile_sketch(): return jnp.dot(affinity, probe_tile, preferred_element_type=jnp.float32)  19.1 us
    another operation x3, other arithmetic, shards(): factor_low = jnp.linalg.cholesky(gram_sum)  12.4 us
    another operation x1, other arithmetic, shards(): jax.scipy.linalg.solve_triangular(factor_low, row_share.T, lower=True)  9.81 us
  transfers between devices with their start and end apart: 3, of which 3 were waited for; matrix products, arithmetic and copies ran while one was open for 2% of the time, Pallas kernels for 0%

commit v1 on v0

v1 whole, which is shorter than its diff:
```python
import functools

import jax
import jax.numpy as jnp
from jax import lax
from jax.experimental import pallas as pl
from jax.experimental.pallas import tpu as pltpu
from jax.sharding import PartitionSpec as P


RING = 16
OWN, FAR = 14, 15
SIDE = 128
HALF = 64
BLK = 1024
MESH = pl.DeviceIdType.MESH
LOG2E = 1.4426950408889634
F32 = jnp.float32
BF16 = jnp.bfloat16
RINGS = 3


def offset_of(slot):
    if slot == OWN:
        return 0
    if slot == FAR:
        return 8
    distance = slot // 2 + 1
    return -distance if slot % 2 == 0 else distance


def slot_of_offset(offset):
    offset %= RING
    if offset == 0:
        return OWN
    if offset == 8:
        return FAR
    return 2 * (RING - offset - 1) if offset > 8 else 2 * (offset - 1) + 1


def unit_rows(block):
    wide = block.astype(F32)
    total = jnp.sum(wide * wide, axis=1, keepdims=True)
    return (wide * lax.rsqrt(total + 1e-06)).astype(BF16)


def sketch_kernel(
    row_ref, rscale_ref, col_ref, cscale_ref, probe_ref, pair_ref,
    sketch_ref, gram_ref,
    rows, cols, stage, raux, bvec, mstack, cmat, ascale, acc, landed, gsrc, g1, g2, g3,
    local_sem, ring_send, ring_recv, sib_send, sib_recv, raux_send, raux_recv, caux_send, caux_recv,
    red_send, red_recv, d1_send, d1_recv, d2_send, d2_recv, d3_send, d3_recv,
):
    r = lax.axis_index("row")
    z = lax.axis_index("col")
    core = lax.rem(r, 2)
    p = r // 2
    x = p // 4
    y = lax.rem(p, 4)
    diag = lax.rem(x + y, 4)
    pos = (4 * x + diag, 4 * y + diag)

    def chip_at(ring, place):
        place = lax.rem(place + 2 * RING, RING)
        a = place // 4
        b = lax.rem(place - a + 8, 4)
        return 4 * a + b if ring == 0 else 4 * b + a

    def device_at(ring, offset):
        if ring == 2:
            return (r, lax.rem(z + offset + RING, RING))
        return (2 * chip_at(ring, pos[ring] + offset) + core, z)

    sibling = (2 * p + 1 - core, z)

    barrier = pltpu.get_barrier_semaphore()

    def greet_plane(i, carry):
        pl.semaphore_signal(
            barrier, inc=1, device_id=(lax.rem(r + i, 32), z), device_id_type=MESH
        )
        return carry

    def greet_ring(i, carry):
        pl.semaphore_signal(
            barrier, inc=1, device_id=(r, lax.rem(z + i, RING)), device_id_type=MESH
        )
        return carry

    lax.fori_loop(1, 32, greet_plane, 0)
    lax.fori_loop(1, RING, greet_ring, 0)

    start = pl.multiple_of(p * SIDE, SIDE)
    col_copy = pltpu.make_async_copy(col_ref.at[pl.ds(start, SIDE)], stage, local_sem.at[0])
    probe_copy = pltpu.make_async_copy(
        probe_ref.at[pl.ds(start, SIDE)], cols.at[OWN, :, pl.ds(1024, SIDE)], local_sem.at[1]
    )
    col_copy.start()
    probe_copy.start()
    rows[OWN] = unit_rows(row_ref[...])
    lane = lax.broadcasted_iota(jnp.int32, (1, SIDE), 1)
    block_row = z // 8
    mask = jnp.zeros((1, SIDE), F32)
    for s in range(pair_ref.shape[1]):
        mask = jnp.where(lane == pair_ref[block_row, s], 1.0, mask)
    raux[p, 0:1, :] = (2.0 * LOG2E) / rscale_ref[pl.ds(z, 1), :]
    raux[p, 1:2, :] = mask
    bvec[OWN] = 1.0 / cscale_ref[pl.ds(p, 1), :]
    col_copy.wait()
    cols[OWN, :, :1024] = unit_rows(stage[...])
    probe_copy.wait()
    pl.semaphore_wait(barrier, 46)

    half = pl.ds(pl.multiple_of(core * HALF, HALF), HALF)

    def ring_copy(ring, way, step):
        source = OWN if step == 1 else 2 * (step - 2) + way
        target = FAR if step == 8 else 2 * (step - 1) + way
        low, count = (0, HALF) if step < 8 else (way * HALF // 2, HALF // 2)
        if ring == 2:
            part = pl.ds(pl.multiple_of(core * HALF + low, HALF // 2), count)
            buffer = cols
        else:
            part = pl.ds(ring * HALF + low, count)
            buffer = rows
        return pltpu.make_async_remote_copy(
            src_ref=buffer.at[source, part],
            dst_ref=buffer.at[target, part],
            send_sem=ring_send.at[ring, way, step - 1],
            recv_sem=ring_recv.at[ring, way, step - 1],
            device_id=device_at(ring, 1 - 2 * way),
            device_id_type=MESH,
        )

    def sibling_copy(step):
        first, count = (2 * (step - 1), 2) if step < 8 else (FAR, 1)
        return pltpu.make_async_remote_copy(
            src_ref=cols.at[pl.ds(first, count), half],
            dst_ref=cols.at[pl.ds(first, count), half],
            send_sem=sib_send.at[step - 1],
            recv_sem=sib_recv.at[step - 1],
            device_id=sibling,
            device_id_type=MESH,
        )

    sent = {}
    for ring in range(RINGS):
        for way in range(2):
            sent[ring, way, 1] = ring_copy(ring, way, 1)
            sent[ring, way, 1].start()

    def raux_copy(i):
        other = lax.rem(p + i, RING)
        return pltpu.make_async_remote_copy(
            src_ref=raux.at[p],
            dst_ref=raux.at[p],
            send_sem=raux_send.at[i],
            recv_sem=raux_recv.at[p],
            device_id=(2 * other + core, z),
            device_id_type=MESH,
        )

    def raux_arrival(i):
        other = lax.rem(p + i, RING)
        return pltpu.make_async_remote_copy(
            src_ref=raux.at[other],
            dst_ref=raux.at[other],
            send_sem=raux_send.at[i],
            recv_sem=raux_recv.at[other],
            device_id=(2 * other + core, z),
            device_id_type=MESH,
        )

    def caux_copy(offset):
        target = slot_of_offset(-offset)
        return pltpu.make_async_remote_copy(
            src_ref=bvec.at[OWN],
            dst_ref=bvec.at[target],
            send_sem=caux_send.at[target],
            recv_sem=caux_recv.at[target],
            device_id=device_at(2, offset),
            device_id_type=MESH,
        )

    def each(count, act):
        def body(i, carry):
            act(i)
            return carry

        lax.fori_loop(1, count, body, 0)

    each(RING, lambda i: raux_copy(i).start())
    caux = [caux_copy(offset) for offset in range(1, RING)]
    for copy in caux:
        copy.start()

    def prepare():
        each(RING, lambda i: raux_arrival(i).wait_recv())
        for copy in caux:
            copy.wait_recv()
        eye = lax.broadcasted_iota(jnp.int32, (SIDE, SIDE), 0) == lax.broadcasted_iota(
            jnp.int32, (SIDE, SIDE), 1
        )
        for slot in range(RING):
            first = raux[chip_at(0, pos[0] + offset_of(slot))]
            second = raux[chip_at(1, pos[1] + offset_of(slot))]
            mstack[2 * slot : 2 * slot + 1, :] = first[1:2]
            mstack[2 * slot + 1 : 2 * slot + 2, :] = second[1:2]
            scale = jnp.where(lane < HALF, first[0:1], second[0:1])
            column = jnp.sum(jnp.where(eye, scale, 0.0), axis=1, keepdims=True)
            ascale[slot * SIDE : (slot + 1) * SIDE, :] = jnp.broadcast_to(column, (SIDE, SIDE))
        width = RING * SIDE
        slot_at = lax.broadcasted_iota(jnp.int32, (SIDE, width), 1) // SIDE
        step_at = slot_at // 2 + 1
        shift = jnp.where(slot_at == 2 * (step_at - 1), -step_at, step_at)
        shift = jnp.where(slot_at == OWN, 0, shift)
        shift = jnp.where(slot_at == FAR, 8, shift)
        plane_at = (shift + z + RING) & (RING - 1)
        wanted = lax.broadcasted_iota(jnp.int32, (SIDE, width), 0) == 2 * plane_at + p // 8
        chosen = jnp.dot(
            mstack[...].astype(BF16), wanted.astype(F32).astype(BF16), preferred_element_type=F32
        )
        cmat[...] = (1.0 - chosen) * 1e30 + 1.0

    def tile(r0, m, c0, n):
        lhs = rows[r0 : r0 + m].reshape(m * SIDE, 1024)
        rhs = cols[c0 : c0 + n, :, :1024].reshape(n * SIDE, 1024)
        cosine = lax.dot_general(
            lhs, rhs, (((1,), (1,)), ((), ())), preferred_element_type=F32
        )
        inverse = jnp.concatenate([bvec[c] for c in range(c0, c0 + n)], axis=1)
        parts = []
        for piece in range(2 * m):
            at = 2 * r0 + piece
            shifted = (
                cosine[piece * HALF : (piece + 1) * HALF]
                - cmat[at : at + 1, c0 * SIDE : (c0 + n) * SIDE]
            )
            power = shifted * inverse * ascale[at * HALF : (at + 1) * HALF, :1]
            parts.append(jnp.exp2(power).astype(BF16))
        affinity = jnp.concatenate(parts, axis=0)
        probes = cols[c0 : c0 + n, :, 1024:].reshape(n * SIDE, SIDE)
        return jnp.dot(affinity, probes, preferred_element_type=F32).reshape(m, SIDE, SIDE)

    def add_rows(q):
        acc[2 * q : 2 * q + 2] = tile(2 * q, 2, 0, 2 * q + 2)

    def add_cols(low, high, q):
        if high > low:
            span = slice(2 * low, 2 * high)
            acc[span] = acc[span] + tile(2 * low, 2 * (high - low), 2 * q, 2)

    siblings = {}
    for step in range(1, 9):
        if step == 2:
            prepare()
        if step >= 2:
            siblings[step - 1].wait_recv()
            add_rows(step - 2)
            add_cols(0, step - 2, step - 2)
        for ring in range(RINGS):
            for way in range(2):
                sent[ring, way, step].wait_recv()
                if step < 8:
                    sent[ring, way, step + 1] = ring_copy(ring, way, step + 1)
                    sent[ring, way, step + 1].start()
        siblings[step] = sibling_copy(step)
        siblings[step].start()
    siblings[8].wait_recv()

    reduces = []

    def send_back(slot):
        for ring in range(2):
            index = slot if slot < OWN else OWN
            part = pl.ds(ring * HALF, HALF)
            copy = pltpu.make_async_remote_copy(
                src_ref=acc.at[slot, part],
                dst_ref=landed.at[index, part],
                send_sem=red_send.at[index, ring],
                recv_sem=red_recv.at[index, ring],
                device_id=device_at(ring, offset_of(slot)),
                device_id_type=MESH,
            )
            copy.start()
            reduces.append(copy)

    add_rows(7)
    send_back(FAR)
    add_cols(0, 4, 7)
    for slot in range(8):
        send_back(slot)
    add_cols(4, 7, 7)
    for slot in range(8, OWN):
        send_back(slot)
    for copy in reduces:
        copy.wait_recv()
    total = acc[OWN]
    for index in range(RING - 1):
        total = total + landed[index]
    sketch_ref[...] = total

    gram = lax.dot_general(
        total, total, (((0,), (0,)), ((), ())),
        precision=lax.Precision.HIGHEST, preferred_element_type=F32,
    )
    gsrc[...] = gram.reshape(RING, 8, SIDE)

    def d1_copy(i):
        other = lax.rem(r + i, 32)
        return pltpu.make_async_remote_copy(
            src_ref=gsrc.at[other // 2],
            dst_ref=g1.at[r],
            send_sem=d1_send.at[i],
            recv_sem=d1_recv.at[r],
            device_id=(other, z),
            device_id_type=MESH,
        )

    def d1_arrival(i):
        other = lax.rem(r + i, 32)
        return pltpu.make_async_remote_copy(
            src_ref=gsrc.at[0],
            dst_ref=g1.at[other],
            send_sem=d1_send.at[i],
            recv_sem=d1_recv.at[other],
            device_id=(other, z),
            device_id_type=MESH,
        )

    each(32, lambda i: d1_copy(i).start())
    g1[r] = gsrc[p]
    each(32, lambda i: d1_arrival(i).wait_recv())
    g2[z] = jnp.sum(g1[...], axis=0)

    def d2_copy(i, mine):
        other = lax.rem(z + i, RING)
        at = z if mine else other
        return pltpu.make_async_remote_copy(
            src_ref=g2.at[at],
            dst_ref=g2.at[at],
            send_sem=d2_send.at[i],
            recv_sem=d2_recv.at[at],
            device_id=(r, other),
            device_id_type=MESH,
        )

    each(RING, lambda i: d2_copy(i, True).start())
    each(RING, lambda i: d2_copy(i, False).wait_recv())
    g3[p] = jnp.sum(g2[...], axis=0)

    def d3_copy(i, mine):
        other = lax.rem(p + i, RING)
        at = p if mine else other
        return pltpu.make_async_remote_copy(
            src_ref=g3.at[at],
            dst_ref=g3.at[at],
            send_sem=d3_send.at[i],
            recv_sem=d3_recv.at[at],
            device_id=(2 * other + core, z),
            device_id_type=MESH,
        )

    each(RING, lambda i: d3_copy(i, True).start())
    each(RING, lambda i: d3_copy(i, False).wait_recv())
    gram_ref[...] = g3[...].reshape(SIDE, SIDE) * (1.0 / 65536.0)

    for copy in sent.values():
        copy.wait_send()
    for copy in siblings.values():
        copy.wait_send()
    for copy in reduces:
        copy.wait_send()
    for copy in caux:
        copy.wait_send()
    each(RING, lambda i: raux_copy(i).wait_send())
    each(32, lambda i: d1_copy(i).wait_send())
    each(RING, lambda i: d2_copy(i, True).wait_send())
    each(RING, lambda i: d3_copy(i, True).wait_send())


def sketch_and_gram(row_desc, row_scale, col_desc, col_scale, probe, pair_list):
    vmem = pl.BlockSpec(memory_space=pltpu.VMEM)
    hbm = pl.BlockSpec(memory_space=pl.ANY)
    smem = pl.BlockSpec(memory_space=pltpu.SMEM)
    dma = pltpu.SemaphoreType.DMA
    square = jax.ShapeDtypeStruct((SIDE, SIDE), F32)
    return pl.pallas_call(
        sketch_kernel,
        name="sketch_and_gram",
        out_shape=(square, square),
        in_specs=[vmem, vmem, hbm, vmem, hbm, smem],
        out_specs=(vmem, vmem),
        scratch_shapes=[
            pltpu.VMEM((RING, SIDE, 1024), BF16),
            pltpu.VMEM((RING, SIDE, 1024 + SIDE), BF16),
            pltpu.VMEM((SIDE, 1024), BF16),
            pltpu.VMEM((RING, 2, SIDE), F32),
            pltpu.VMEM((RING, 1, SIDE), F32),
            pltpu.VMEM((2 * RING, SIDE), F32),
            pltpu.VMEM((2 * RING, RING * SIDE), F32),
            pltpu.VMEM((RING * SIDE, SIDE), F32),
            pltpu.VMEM((RING, SIDE, SIDE), F32),
            pltpu.VMEM((RING - 1, SIDE, SIDE), F32),
            pltpu.VMEM((RING, 8, SIDE), F32),
            pltpu.VMEM((32, 8, SIDE), F32),
            pltpu.VMEM((RING, 8, SIDE), F32),
            pltpu.VMEM((RING, 8, SIDE), F32),
            dma((2,)),
            dma((RINGS, 2, 8)),
            dma((RINGS, 2, 8)),
            dma((8,)),
            dma((8,)),
            dma((RING,)),
            dma((RING,)),
            dma((RING,)),
            dma((RING,)),
            dma((RING - 1, 2)),
            dma((RING - 1, 2)),
            dma((32,)),
            dma((32,)),
            dma((RING,)),
            dma((RING,)),
            dma((RING,)),
            dma((RING,)),
        ],
        compiler_params=pltpu.CompilerParams(
            collective_id=0, has_side_effects=True, vmem_limit_bytes=56 << 20
        ),
    )(
        row_desc,
        row_scale.reshape(RING, SIDE),
        col_desc,
        col_scale.astype(F32).reshape(RING, SIDE),
        probe,
        pair_list,
    )


def shards(row_desc, row_scale, col_desc, col_scale, probe, pair_list):
    sketch, gram = sketch_and_gram(row_desc, row_scale, col_desc, col_scale, probe, pair_list)
    factor_low = jnp.linalg.cholesky(gram)
    basis_out = jax.scipy.linalg.solve_triangular(factor_low, sketch.T, lower=True).T
    return (basis_out, factor_low.T)


def solution(mesh):
    return jax.shard_map(
        shards,
        mesh=mesh,
        in_specs=(
            P(("row", "col"), None),
            P("row"),
            P("col", None),
            P("col"),
            P("col", None),
            P("row", None),
        ),
        out_specs=(P(("row", "col"), None), P()),
        check_vma=False,
    )
```

time: 420 us -> 127 us (0.30)
  waiting for transfers between devices: 335 us -> 0 us
  Pallas kernels: 0 us -> 97.5 us
  matrix products: 24.7 us -> 1.68 us
  between operations: 13.8 us -> 0.67 us
  other arithmetic: 34.5 us -> 25 us
  local copies, waits for them, and re-layouts: 8.65 us -> 1.66 us
    psum x2 -> x0, waiting for transfers between devices: 267 us -> none  [the longest x1 134 us: shards(): summed = lax.psum(sketch, 'col')]
    pallas_call x0 -> x1, Pallas kernels: none -> 97.5 us  [sketch_and_gram(): pl.pallas_call(sketch_kernel, name='sketch_and_gram', out_shape=(square,...]
    all_gather x1 -> x0, waiting for transfers between devices: 68.2 us -> none  [shards(): gathered = lax.all_gather(row_unit, 'col', axis=0, tiled=True)]
    dot_general x5 -> x0, matrix products: 23.1 us -> none  [the longest x4 19.1 us: tile_sketch(): return jnp.dot(affinity, probe_tile, preferred_element_type=jnp.float32)]
    dynamic_slice x6 -> x0, local copies, waits for them, and re-layouts: 4.88 us -> none  [the longest x2 3.54 us: one_block(): row_tile = lax.dynamic_slice_in_dim(gathered, offset, BLK, 0)]
    convert_element_type x4 -> x0, other arithmetic: 4.52 us -> none  [the longest x2 4.51 us: unit_rows(): return (widened * lax.rsqrt(total + 1e-06)).astype(jnp.bfloat16)]
    reduce_sum x2 -> x0, other arithmetic: 4.4 us -> none  [unit_rows(): total = jnp.sum(widened * widened, axis=1, keepdims=True)]
  transfers between devices with their start and end apart: 3 -> 0, of which waited for: 3 -> 0; matrix products, arithmetic and copies ran while one was open for 2% -> 0% of each run, Pallas kernels for 0% -> 0%
where the time goes in v1:
time: 127 us
  Pallas kernels  97.5 us (77%)
  other arithmetic  25 us (20%)
  matrix products  1.68 us (1%)
  local copies, waits for them, and re-layouts  1.66 us (1%)
    pallas_call x1, Pallas kernels, sketch_and_gram(): pl.pallas_call(sketch_kernel, name='sketch_and_gram', out_shape=(square,...  97.5 us
    another operation x3, other arithmetic, shards(): factor_low = jnp.linalg.cholesky(gram)  12.4 us
    another operation x1, other arithmetic, shards(): jax.scipy.linalg.solve_triangular(factor_low, sketch.T, lower=True)  9.81 us

profile of v1, /device:TPU:1, one launch (start us, length us, event | category | flops | bytes accessed | tf_op | source)
XLA Modules:
  0.0 126.5 jit_solution(7541919486897493434)
XLA Ops:
  0.6 1.3 %bitcast_convert_fusion.cscale_ref = f32[16,128]{1,0:T(8,128)} fusion(bf16[2048]{0:T(1024)(128)(2,1)} %param.9), kind=kLoop, calls=%fused_computation.10 | loop fusion | flops 2048 | bytes 12288 | tf_op jit(solution)/shard_map/reshape | solution.py:434
  1.9 97.5 %sketch_and_gram.1 = (f32[128,128]{1,0:T(8,128)}, f32[128,128]{1,0:T(8,128)}) custom-call(bf16[128,1024]{1,0:T(8,128)(2,1)} %row_ref.1, f32[16,128]{1,0:T(8,128)} %bitcast.16, bf16[2048,1024]{1,0:T(8,128)(2,1)} %col_ref.1, f32[16,128]{1,0:T(8,128)} %bitcast_convert_fusion.cscale_ref, bf16[2048,128]{1,0:T(8,128)(2,1)} %probe_ref.1, s32[2,24]{1,0:T(2,128)} %pair_ref.1), custom_call_target="tpu_custom_call" | custom-call | tf_op jit(solution)/shard_map/sketch_and_gram/pallas_call | solution.py:388
  99.5 0.9 copy.8
  100.4 0.9 fusion.2
  101.3 11.7 %cholesky.16 = f32[128,128]{1,0:T(8,128)S(1)} custom-call(f32[128,128]{1,0:T(8,128)S(1)} %fusion.2), custom_call_target="Cholesky" | custom-call | tf_op jit(solution)/shard_map/jit(cholesky)/cholesky | solution.py:442
  113.0 0.6 compare_reduce_fusion
  113.7 0.7 fusion.3
  114.3 0.7 copy.9
  115.0 9.8 %custom-call.7 = f32[1,128,128]{1,2,0:T(8,128)S(1)} custom-call(f32[1,128,128]{2,1,0:T(8,128)S(1)} %get-tuple-element.9), custom_call_target="InvertDiagBlocksLowerTriangular" | custom-call | tf_op jit(solution)/shard_map/jit(_solve_triangular)/triangular_solve | solution.py:443
  124.9 1.7 %fusion = f32[128,128]{1,0:T(8,128)} fusion(f32[128,128]{1,0:T(8,128)} %get-tuple-element.4, f32[1,128,128]{1,2,0:T(8,128)S(1)} %custom-call.7), kind=kOutput, calls=%fused_computation | convolution fusion | flops 25165824 | bytes 196608 | tf_op jit(solution)/shard_map/jit(_solve_triangular)/triangular_solve | solution.py:443
  (1 shorter events, 0.0 us)

commit v2 on v1

--- a/solution.py
+++ b/solution.py
@@ -12,7 +12,8 @@
 OWN, FAR = 14, 15
 SIDE = 128
 HALF = 64
-BLK = 1024
+QUARTER = 32
+PANEL = 16
 MESH = pl.DeviceIdType.MESH
 LOG2E = 1.4426950408889634
 F32 = jnp.float32
@@ -45,9 +46,9 @@
 
 
 def sketch_kernel(
-    row_ref, rscale_ref, col_ref, cscale_ref, probe_ref, pair_ref,
+    row_hbm, rscale_hbm, col_hbm, cscale_hbm, probe_hbm, pair_hbm,
     sketch_ref, gram_ref,
-    rows, cols, stage, raux, bvec, mstack, cmat, ascale, acc, landed, gsrc, g1, g2, g3,
+    rscale, cscale, pairs, wide, rows, cols, stage, raux, bvec, mstack, cmat, ascale, acc, leaving, landed, gsrc, g1, g2, g3,
     local_sem, ring_send, ring_recv, sib_send, sib_recv, raux_send, raux_recv, caux_send, caux_recv,
     red_send, red_recv, d1_send, d1_recv, d2_send, d2_recv, d3_send, d3_recv,
 ):
@@ -87,47 +88,54 @@
         )
         return carry
 
+    start = pl.multiple_of(p * SIDE, SIDE)
+    own = [
+        (row_hbm, stage.at[0]),
+        (col_hbm.at[pl.ds(start, SIDE)], stage.at[1]),
+        (rscale_hbm, rscale),
+        (cscale_hbm, cscale),
+        (pair_hbm, pairs),
+        (probe_hbm.at[pl.ds(start, SIDE)], cols.at[OWN, :, pl.ds(1024, SIDE)]),
+    ]
+    own = [pltpu.make_async_copy(a, b, local_sem.at[i]) for i, (a, b) in enumerate(own)]
+    for copy in own:
+        copy.start()
     lax.fori_loop(1, 32, greet_plane, 0)
     lax.fori_loop(1, RING, greet_ring, 0)
-
-    start = pl.multiple_of(p * SIDE, SIDE)
-    col_copy = pltpu.make_async_copy(col_ref.at[pl.ds(start, SIDE)], stage, local_sem.at[0])
-    probe_copy = pltpu.make_async_copy(
-        probe_ref.at[pl.ds(start, SIDE)], cols.at[OWN, :, pl.ds(1024, SIDE)], local_sem.at[1]
-    )
-    col_copy.start()
-    probe_copy.start()
-    rows[OWN] = unit_rows(row_ref[...])
+    own[0].wait()
+    rows[OWN] = unit_rows(stage[0])
+    own[1].wait()
+    cols[OWN, :, :1024] = unit_rows(stage[1])
+    for copy in own[2:]:
+        copy.wait()
     lane = lax.broadcasted_iota(jnp.int32, (1, SIDE), 1)
     block_row = z // 8
     mask = jnp.zeros((1, SIDE), F32)
-    for s in range(pair_ref.shape[1]):
-        mask = jnp.where(lane == pair_ref[block_row, s], 1.0, mask)
-    raux[p, 0:1, :] = (2.0 * LOG2E) / rscale_ref[pl.ds(z, 1), :]
+    for s in range(pairs.shape[1]):
+        mask = jnp.where(lane == pairs[block_row, s], 1.0, mask)
+    raux[p, 0:1, :] = (2.0 * LOG2E) / rscale[pl.ds(z, 1), :]
     raux[p, 1:2, :] = mask
-    bvec[OWN] = 1.0 / cscale_ref[pl.ds(p, 1), :]
-    col_copy.wait()
-    cols[OWN, :, :1024] = unit_rows(stage[...])
-    probe_copy.wait()
+    wide[...] = cscale[...].astype(F32).reshape(RING, SIDE)
+    bvec[OWN] = 1.0 / wide[pl.ds(p, 1), :]
     pl.semaphore_wait(barrier, 46)
 
     half = pl.ds(pl.multiple_of(core * HALF, HALF), HALF)
 
-    def ring_copy(ring, way, step):
+    def ring_copy(ring, way, step, sub):
         source = OWN if step == 1 else 2 * (step - 2) + way
         target = FAR if step == 8 else 2 * (step - 1) + way
-        low, count = (0, HALF) if step < 8 else (way * HALF // 2, HALF // 2)
+        low = sub * QUARTER
         if ring == 2:
-            part = pl.ds(pl.multiple_of(core * HALF + low, HALF // 2), count)
+            part = pl.ds(pl.multiple_of(core * HALF + low, QUARTER), QUARTER)
             buffer = cols
         else:
-            part = pl.ds(ring * HALF + low, count)
+            part = pl.ds(ring * HALF + low, QUARTER)
             buffer = rows
         return pltpu.make_async_remote_copy(
             src_ref=buffer.at[source, part],
             dst_ref=buffer.at[target, part],
-            send_sem=ring_send.at[ring, way, step - 1],
-            recv_sem=ring_recv.at[ring, way, step - 1],
+            send_sem=ring_send.at[ring, way, step - 1, sub],
+            recv_sem=ring_recv.at[ring, way, step - 1, sub],
             device_id=device_at(ring, 1 - 2 * way),
             device_id_type=MESH,
         )
@@ -144,10 +152,16 @@
         )
 
     sent = {}
-    for ring in range(RINGS):
-        for way in range(2):
-            sent[ring, way, 1] = ring_copy(ring, way, 1)
-            sent[ring, way, 1].start()
+
+    def pass_on(ring, way, step, sub):
+        if step < 8 or sub == way:
+            sent[ring, way, step, sub] = ring_copy(ring, way, step, sub)
+            sent[ring, way, step, sub].start()
+
+    for sub in range(2):
+        for ring in range(RINGS):
+            for way in range(2):
+                pass_on(ring, way, 1, sub)
 
     def raux_copy(i):
         other = lax.rem(p + i, RING)
@@ -250,32 +264,41 @@
             span = slice(2 * low, 2 * high)
             acc[span] = acc[span] + tile(2 * low, 2 * (high - low), 2 * q, 2)
 
+    def take(step, sub):
+        for ring in range(RINGS):
+            for way in range(2):
+                if (ring, way, step, sub) in sent:
+                    sent[ring, way, step, sub].wait_recv()
+                    if step < 8:
+                        pass_on(ring, way, step + 1, sub)
+
     siblings = {}
     for step in range(1, 9):
-        if step == 2:
-            prepare()
-        if step >= 2:
+        take(step, 0)
+        if step >= 3:
             siblings[step - 1].wait_recv()
+            if step == 3:
+                add_rows(0)
             add_rows(step - 2)
-            add_cols(0, step - 2, step - 2)
-        for ring in range(RINGS):
-            for way in range(2):
-                sent[ring, way, step].wait_recv()
-                if step < 8:
-                    sent[ring, way, step + 1] = ring_copy(ring, way, step + 1)
-                    sent[ring, way, step + 1].start()
+        take(step, 1)
         siblings[step] = sibling_copy(step)
         siblings[step].start()
+        if step == 2:
+            siblings[1].wait_recv()
+            prepare()
+        if step >= 3:
+            add_cols(0, step - 2, step - 2)
     siblings[8].wait_recv()
 
     reduces = []
 
     def send_back(slot):
+        index = slot if slot < OWN else OWN
+        leaving[index] = acc[slot].astype(BF16)
         for ring in range(2):
-            index = slot if slot < OWN else OWN
             part = pl.ds(ring * HALF, HALF)
             copy = pltpu.make_async_remote_copy(
-                src_ref=acc.at[slot, part],
+                src_ref=leaving.at[index, part],
                 dst_ref=landed.at[index, part],
                 send_sem=red_send.at[index, ring],
                 recv_sem=red_recv.at[index, ring],
@@ -285,31 +308,29 @@
             copy.start()
             reduces.append(copy)
 
+    for low, high in ((0, 2), (2, 4), (4, 7)):
+        add_cols(low, high, 7)
+        for slot in range(2 * low, 2 * high):
+            send_back(slot)
     add_rows(7)
     send_back(FAR)
-    add_cols(0, 4, 7)
-    for slot in range(8):
-        send_back(slot)
-    add_cols(4, 7, 7)
-    for slot in range(8, OWN):
-        send_back(slot)
     for copy in reduces:
         copy.wait_recv()
     total = acc[OWN]
     for index in range(RING - 1):
-        total = total + landed[index]
+        total = total + landed[index].astype(F32)
     sketch_ref[...] = total
 
     gram = lax.dot_general(
         total, total, (((0,), (0,)), ((), ())),
         precision=lax.Precision.HIGHEST, preferred_element_type=F32,
     )
-    gsrc[...] = gram.reshape(RING, 8, SIDE)
+    gsrc[...] = gram.reshape(32, 4, SIDE)
 
     def d1_copy(i):
         other = lax.rem(r + i, 32)
         return pltpu.make_async_remote_copy(
-            src_ref=gsrc.at[other // 2],
+            src_ref=gsrc.at[other],
             dst_ref=g1.at[r],
             send_sem=d1_send.at[i],
             recv_sem=d1_recv.at[r],
@@ -329,7 +350,7 @@
         )
 
     each(32, lambda i: d1_copy(i).start())
-    g1[r] = gsrc[p]
+    g1[r] = gsrc[r]
     each(32, lambda i: d1_arrival(i).wait_recv())
     g2[z] = jnp.sum(g1[...], axis=0)
 
@@ -347,22 +368,22 @@
 
     each(RING, lambda i: d2_copy(i, True).start())
     each(RING, lambda i: d2_copy(i, False).wait_recv())
-    g3[p] = jnp.sum(g2[...], axis=0)
+    g3[r] = jnp.sum(g2[...], axis=0)
 
     def d3_copy(i, mine):
-        other = lax.rem(p + i, RING)
-        at = p if mine else other
+        other = lax.rem(r + i, 32)
+        at = r if mine else other
         return pltpu.make_async_remote_copy(
             src_ref=g3.at[at],
             dst_ref=g3.at[at],
             send_sem=d3_send.at[i],
             recv_sem=d3_recv.at[at],
-            device_id=(2 * other + core, z),
-            device_id_type=MESH,
-        )
-
-    each(RING, lambda i: d3_copy(i, True).start())
-    each(RING, lambda i: d3_copy(i, False).wait_recv())
+            device_id=(other, z),
+            device_id_type=MESH,
+        )
+
+    each(32, lambda i: d3_copy(i, True).start())
+    each(32, lambda i: d3_copy(i, False).wait_recv())
     gram_ref[...] = g3[...].reshape(SIDE, SIDE) * (1.0 / 65536.0)
 
     for copy in sent.values():
@@ -376,39 +397,43 @@
     each(RING, lambda i: raux_copy(i).wait_send())
     each(32, lambda i: d1_copy(i).wait_send())
     each(RING, lambda i: d2_copy(i, True).wait_send())
-    each(RING, lambda i: d3_copy(i, True).wait_send())
+    each(32, lambda i: d3_copy(i, True).wait_send())
 
 
 def sketch_and_gram(row_desc, row_scale, col_desc, col_scale, probe, pair_list):
     vmem = pl.BlockSpec(memory_space=pltpu.VMEM)
     hbm = pl.BlockSpec(memory_space=pl.ANY)
-    smem = pl.BlockSpec(memory_space=pltpu.SMEM)
     dma = pltpu.SemaphoreType.DMA
     square = jax.ShapeDtypeStruct((SIDE, SIDE), F32)
     return pl.pallas_call(
         sketch_kernel,
         name="sketch_and_gram",
         out_shape=(square, square),
-        in_specs=[vmem, vmem, hbm, vmem, hbm, smem],
+        in_specs=[hbm] * 6,
         out_specs=(vmem, vmem),
         scratch_shapes=[
+            pltpu.VMEM((RING, SIDE), F32),
+            pltpu.VMEM((RING * SIDE,), BF16),
+            pltpu.SMEM((2, 24), jnp.int32),
+            pltpu.VMEM((RING, SIDE), F32),
             pltpu.VMEM((RING, SIDE, 1024), BF16),
             pltpu.VMEM((RING, SIDE, 1024 + SIDE), BF16),
-            pltpu.VMEM((SIDE, 1024), BF16),
+            pltpu.VMEM((2, SIDE, 1024), BF16),
             pltpu.VMEM((RING, 2, SIDE), F32),
             pltpu.VMEM((RING, 1, SIDE), F32),
             pltpu.VMEM((2 * RING, SIDE), F32),
             pltpu.VMEM((2 * RING, RING * SIDE), F32),
             pltpu.VMEM((RING * SIDE, SIDE), F32),
             pltpu.VMEM((RING, SIDE, SIDE), F32),
-            pltpu.VMEM((RING - 1, SIDE, SIDE), F32),
-            pltpu.VMEM((RING, 8, SIDE), F32),
-            pltpu.VMEM((32, 8, SIDE), F32),
-            pltpu.VMEM((RING, 8, SIDE), F32),
-            pltpu.VMEM((RING, 8, SIDE), F32),
-            dma((2,)),
-            dma((RINGS, 2, 8)),
-            dma((RINGS, 2, 8)),
+            pltpu.VMEM((RING - 1, SIDE, SIDE), BF16),
+            pltpu.VMEM((RING - 1, SIDE, SIDE), BF16),
+            pltpu.VMEM((32, 4, SIDE), F32),
+            pltpu.VMEM((32, 4, SIDE), F32),
+            pltpu.VMEM((RING, 4, SIDE), F32),
+            pltpu.VMEM((32, 4, SIDE), F32),
+            dma((6,)),
+            dma((RINGS, 2, 8, 2)),
+            dma((RINGS, 2, 8, 2)),
             dma((8,)),
             dma((8,)),
             dma((RING,)),
@@ -421,8 +446,8 @@
             dma((32,)),
             dma((RING,)),
             dma((RING,)),
-            dma((RING,)),
-            dma((RING,)),
+            dma((32,)),
+            dma((32,)),
         ],
         compiler_params=pltpu.CompilerParams(
             collective_id=0, has_side_effects=True, vmem_limit_bytes=56 << 20
@@ -431,17 +456,69 @@
         row_desc,
         row_scale.reshape(RING, SIDE),
         col_desc,
-        col_scale.astype(F32).reshape(RING, SIDE),
+        col_scale,
         probe,
         pair_list,
     )
 
 
+def factor_kernel(sketch_ref, gram_ref, basis_ref, factor_ref, work):
+    work[:, :SIDE] = gram_ref[...]
+    work[:, SIDE:] = sketch_ref[...].T
+    for base in range(0, SIDE, PANEL):
+        rows = [work[base + i : base + i + 1, :] for i in range(PANEL)]
+        low = [
+            [jnp.broadcast_to(rows[i][:, base + j : base + j + 1], (1, SIDE)) for j in range(i + 1)]
+            for i in range(PANEL)
+        ]
+        root = []
+        for j in range(PANEL):
+            root.append(lax.rsqrt(low[j][j]))
+            for i in range(j + 1, PANEL):
+                low[i][j] = low[i][j] * root[j]
+            for i in range(j + 1, PANEL):
+                for k in range(j + 1, i + 1):
+                    low[i][k] = low[i][k] - low[i][j] * low[k][j]
+        left, right = [], []
+        for i in range(PANEL):
+            a, b = rows[i][:, :SIDE], rows[i][:, SIDE:]
+            for j in range(i):
+                a = a - low[i][j] * left[j]
+                b = b - low[i][j] * right[j]
+            left.append(a * root[i])
+            right.append(b * root[i])
+        work[base : base + PANEL, :SIDE] = jnp.concatenate(left, axis=0)
+        work[base : base + PANEL, SIDE:] = jnp.concatenate(right, axis=0)
+        rest = base + PANEL
+        if rest < SIDE:
+            panel = work[base : base + PANEL, :]
+            work[rest:, :] = work[rest:, :] - lax.dot_general(
+                panel[:, :SIDE], panel, (((0,), (0,)), ((), ())),
+                precision=lax.Precision.HIGHEST, preferred_element_type=F32,
+            )[rest:, :]
+    upper = lax.broadcasted_iota(jnp.int32, (SIDE, SIDE), 1) >= lax.broadcasted_iota(
+        jnp.int32, (SIDE, SIDE), 0
+    )
+    factor_ref[...] = jnp.where(upper, work[:, :SIDE], 0.0)
+    basis_ref[...] = work[:, SIDE:].T
+
+
+def factor_and_solve(sketch, gram):
+    vmem = pl.BlockSpec(memory_space=pltpu.VMEM)
+    square = jax.ShapeDtypeStruct((SIDE, SIDE), F32)
+    return pl.pallas_call(
+        factor_kernel,
+        name="factor_and_solve",
+        out_shape=(square, square),
+        in_specs=[vmem, vmem],
+        out_specs=(vmem, vmem),
+        scratch_shapes=[pltpu.VMEM((SIDE, 2 * SIDE), F32)],
+    )(sketch, gram)
+
+
 def shards(row_desc, row_scale, col_desc, col_scale, probe, pair_list):
     sketch, gram = sketch_and_gram(row_desc, row_scale, col_desc, col_scale, probe, pair_list)
-    factor_low = jnp.linalg.cholesky(gram)
-    basis_out = jax.scipy.linalg.solve_triangular(factor_low, sketch.T, lower=True).T
-    return (basis_out, factor_low.T)
+    return factor_and_solve(sketch, gram)
 
 
 def solution(mesh):

time: 127 us -> 97.4 us (0.77)
  other arithmetic: 25 us -> 0 us
  matrix products: 1.68 us -> 0 us
  local copies, waits for them, and re-layouts: 1.66 us -> 0 us
    another operation x4 -> x0, other arithmetic: 22.2 us -> none  [the longest x3 12.4 us: shards(): factor_low = jnp.linalg.cholesky(gram)]
    pallas_call x1, Pallas kernels: 97.5 us -> 89.1 us  [sketch_and_gram(): pl.pallas_call(sketch_kernel, name='sketch_and_gram', out_shape=(square,...]
    pallas_call x0 -> x1, Pallas kernels: none -> 7.49 us  [factor_and_solve(): pl.pallas_call(factor_kernel, name='factor_and_solve', out_shape=(square,...]
    another operation x1 -> x0, matrix products: 1.68 us -> none  [shards(): jax.scipy.linalg.solve_triangular(factor_low, sketch.T, lower=True)]
    reshape x1 -> x0, other arithmetic: 1.29 us -> none  [sketch_and_gram(): col_scale.astype(F32).reshape(RING, SIDE)]
where the time goes in v2:
time: 97.4 us; the launch traced here: 97.2 us
  Pallas kernels  96.6 us (99%)
    pallas_call x1, Pallas kernels, sketch_and_gram(): pl.pallas_call(sketch_kernel, name='sketch_and_gram', out_shape=(square,...  89.1 us
    pallas_call x1, Pallas kernels, factor_and_solve(): pl.pallas_call(factor_kernel, name='factor_and_solve', out_shape=(square,...  7.49 us

profile of v2, /device:TPU:1, one launch (start us, length us, event | category | flops | bytes accessed | tf_op | source)
XLA Modules:
  0.0 97.2 jit_solution(7422135696712311767)
XLA Ops:
  0.6 89.1 %sketch_and_gram.1 = (f32[128,128]{1,0:T(8,128)}, f32[128,128]{1,0:T(8,128)}) custom-call(bf16[128,1024]{1,0:T(8,128)(2,1)} %row_hbm.1, f32[16,128]{1,0:T(8,128)} %bitcast.1, bf16[2048,1024]{1,0:T(8,128)(2,1)} %col_hbm.1, bf16[2048]{0:T(1024)(128)(2,1)} %cscale_hbm.1, bf16[2048,128]{1,0:T(8,128)(2,1)} %probe_hbm.1, s32[2,24]{1,0:T(2,128)} %pair_hbm.1), custom_call_target="tpu_custom_call" | custom-call | tf_op jit(solution)/shard_map/sketch_and_gram/pallas_call | solution.py:408
  89.7 7.5 %factor_and_solve.1 = (f32[128,128]{1,0:T(8,128)}, f32[128,128]{1,0:T(8,128)}) custom-call(f32[128,128]{1,0:T(8,128)} %get-tuple-element.4.sketch_ref, f32[128,128]{1,0:T(8,128)} %get-tuple-element.5.gram_ref), custom_call_target="tpu_custom_call" | custom-call | tf_op jit(solution)/shard_map/factor_and_solve/pallas_call | solution.py:509

commit v3 on v2

--- a/solution.py
+++ b/solution.py
@@ -314,10 +314,13 @@
             send_back(slot)
     add_rows(7)
     send_back(FAR)
-    for copy in reduces:
-        copy.wait_recv()
+    for copy in [*sent.values(), *siblings.values(), *caux]:
+        copy.wait_send()
+    each(RING, lambda i: raux_copy(i).wait_send())
     total = acc[OWN]
     for index in range(RING - 1):
+        for copy in reduces[2 * index : 2 * index + 2]:
+            copy.wait_recv()
         total = total + landed[index].astype(F32)
     sketch_ref[...] = total
 
@@ -350,6 +353,8 @@
         )
 
     each(32, lambda i: d1_copy(i).start())
+    for copy in reduces:
+        copy.wait_send()
     g1[r] = gsrc[r]
     each(32, lambda i: d1_arrival(i).wait_recv())
     g2[z] = jnp.sum(g1[...], axis=0)
@@ -367,6 +372,7 @@
         )
 
     each(RING, lambda i: d2_copy(i, True).start())
+    each(32, lambda i: d1_copy(i).wait_send())
     each(RING, lambda i: d2_copy(i, False).wait_recv())
     g3[r] = jnp.sum(g2[...], axis=0)
 
@@ -383,20 +389,10 @@
         )
 
     each(32, lambda i: d3_copy(i, True).start())
+    each(RING, lambda i: d2_copy(i, True).wait_send())
     each(32, lambda i: d3_copy(i, False).wait_recv())
     gram_ref[...] = g3[...].reshape(SIDE, SIDE) * (1.0 / 65536.0)
 
-    for copy in sent.values():
-        copy.wait_send()
-    for copy in siblings.values():
-        copy.wait_send()
-    for copy in reduces:
-        copy.wait_send()
-    for copy in caux:
-        copy.wait_send()
-    each(RING, lambda i: raux_copy(i).wait_send())
-    each(32, lambda i: d1_copy(i).wait_send())
-    each(RING, lambda i: d2_copy(i, True).wait_send())
     each(32, lambda i: d3_copy(i, True).wait_send())
 
 

time: 97.4 us -> 96.8 us (level)
  no operation moved by 1% of the time
where the time goes in v3:
time: 96.8 us; the launch traced here: 96.6 us
  Pallas kernels  96 us (99%)
    pallas_call x1, Pallas kernels, sketch_and_gram(): pl.pallas_call(sketch_kernel, name='sketch_and_gram', out_shape=(square,...  88.5 us
    pallas_call x1, Pallas kernels, factor_and_solve(): pl.pallas_call(factor_kernel, name='factor_and_solve', out_shape=(square,...  7.48 us

profile of v3, /device:TPU:1, one launch (start us, length us, event | category | flops | bytes accessed | tf_op | source)
XLA Modules:
  0.0 96.6 jit_solution(8828253614396935756)
XLA Ops:
  0.6 88.5 %sketch_and_gram.1 = (f32[128,128]{1,0:T(8,128)}, f32[128,128]{1,0:T(8,128)}) custom-call(bf16[128,1024]{1,0:T(8,128)(2,1)} %row_hbm.1, f32[16,128]{1,0:T(8,128)} %bitcast.1, bf16[2048,1024]{1,0:T(8,128)(2,1)} %col_hbm.1, bf16[2048]{0:T(1024)(128)(2,1)} %cscale_hbm.1, bf16[2048,128]{1,0:T(8,128)(2,1)} %probe_hbm.1, s32[2,24]{1,0:T(2,128)} %pair_hbm.1), custom_call_target="tpu_custom_call" | custom-call | tf_op jit(solution)/shard_map/sketch_and_gram/pallas_call | solution.py:404
  89.1 7.5 %factor_and_solve.1 = (f32[128,128]{1,0:T(8,128)}, f32[128,128]{1,0:T(8,128)}) custom-call(f32[128,128]{1,0:T(8,128)} %get-tuple-element.4.sketch_ref, f32[128,128]{1,0:T(8,128)} %get-tuple-element.5.gram_ref), custom_call_target="tpu_custom_call" | custom-call | tf_op jit(solution)/shard_map/factor_and_solve/pallas_call | solution.py:505
